TPU v7x, 32 devices: a whole 2x2x4 slice. The times are simulated.
32 devices in a mesh: groups: 2 (over y), lat: 4 (over z), mesh: 2 (over x), feat: 2 (over core).
Axes of the slice: x: 2, y: 2, z: 4, core: 2. Of those that a mesh axis runs over, the one named last changes fastest.
Arguments:
- grid_in: bfloat16 [8192, 512], P(('groups', 'lat', 'mesh'), 'feat'), parts along dimension 0, may hold values from -6 to 6
- mesh_in: bfloat16 [2048, 512], P(('groups', 'mesh'), 'feat'), parts along dimension 0, may hold values from -6 to 6
- w_enc: bfloat16 [512, 512], P(None, 'feat'), may hold values from -0.25 to 0.25
- w_proc: bfloat16 [512, 512], P(None, 'feat'), may hold values from -0.25 to 0.25
- w_dec: bfloat16 [512, 512], P(None, 'feat'), may hold values from -0.25 to 0.25
- enc_dst: int32 [8192, 4], P(('groups', 'lat', 'mesh')), parts along dimension 0, may hold values from 0 to 1023, as said below
- enc_count: int32 [8192], P(('groups', 'lat', 'mesh')), parts along dimension 0, may hold values from 1 to 4
- dec_src: int32 [8192, 3], P(('groups', 'lat', 'mesh')), parts along dimension 0, may hold values from 0 to 1023, as said below
- proc_src: int32 [2048, 6], P(('groups', 'mesh')), parts along dimension 0, may hold values from 0 to 1023
- cotangent: bfloat16 [8192, 512], P(('groups', 'lat', 'mesh'), 'feat'), parts along dimension 0, may hold values from -1.5 to 1.5
Outputs:
- grad_grid: bfloat16 [8192, 512], P(('groups', 'lat', 'mesh'), 'feat'), parts along dimension 0
- grad_mesh: bfloat16 [2048, 512], P(('groups', 'mesh'), 'feat'), parts along dimension 0
- grad_w_enc: float32 [1024, 512], P('groups', 'feat'), parts along dimension 0
- grad_w_proc: float32 [1024, 512], P('groups', 'feat'), parts along dimension 0
- grad_w_dec: float32 [1024, 512], P('groups', 'feat'), parts along dimension 0
There are 2 independent parts, one for each index of `groups`. A program takes and returns all parts, laid end to end along the dimension named above; an argument that names none is the same for every part. Nothing has to cross between parts.
Inputs may be any that keep to these rules, and one draw needn't show every extreme that they name: `enc_dst`: number the latitude homes h = l * 2 + m for l < 4, m < 2; home h holds mesh nodes m * 512 + l * 128 + j for j < 128. Grid node g lies in band b = g // 512, and each of its encoder slots names a node of home b - 1, b or b + 1. `dec_src`: each source of grid node g names a node of home b - 1, b or b + 1, with homes and bands numbered as for enc_dst.
All inputs are finite; a program needn't handle non-finite values.
Results may differ from a plain program's by a relative error of at most 0.019.
Values may be sent and summed in bfloat16 or wider, within the bound.
A program may use at most 64 MiB of HBM per device.

v0:
```python
import jax
import jax.numpy as jnp
from jax import lax
from jax.sharding import PartitionSpec as P

KE = 4
KD = 3
KP = 6


def with_halo(value, sides, width):
    for axis, dim in sides:
        size, length = (lax.axis_size(axis), value.shape[dim])
        up = [(i, (i + 1) % size) for i in range(size - 1)]
        down = [(j, i) for i, j in up]
        last = lax.slice_in_dim(value, length - width, length, axis=dim)
        first = lax.slice_in_dim(value, 0, width, axis=dim)
        before = lax.ppermute(last, axis, up)
        after = lax.ppermute(first, axis, down)
        value = jnp.concatenate([before, value, after], axis=dim)
    return value


def silu_grad(pre):
    sig = jax.nn.sigmoid(pre)
    return sig * (1.0 + pre * (1.0 - sig))


def window_slots(targets, is_valid, shard_rows, home_rows, n_mesh, band_index):
    owner_shard = targets // shard_rows
    inner_row = targets % shard_rows
    home_id = inner_row // home_rows * n_mesh + owner_shard
    slot_ids = (home_id - band_index + 1) * home_rows + inner_row % home_rows
    return jnp.where(is_valid, slot_ids, -1)


def window_matrix(slot_ids, win_rows):
    row_ids = jnp.arange(win_rows, dtype=jnp.int32)[:, None]
    matrix = jnp.zeros((win_rows, slot_ids.shape[0]), jnp.bfloat16)
    for column in range(slot_ids.shape[1]):
        matrix = matrix + (row_ids == slot_ids[:, column][None, :]).astype(jnp.bfloat16)
    return matrix


def band_sum(window, home_rows):
    stacked = window.reshape(3, home_rows, window.shape[1])
    padded_win = with_halo(stacked.astype(jnp.bfloat16), ((("lat", "mesh"), 0),), 3).astype(
        stacked.dtype
    )
    return padded_win[2] + padded_win[4] + padded_win[6]


def collect_rows(home_block):
    return lax.all_gather(home_block, "lat", axis=0, tiled=True)


def widen(latent):
    return lax.all_gather(latent, "feat", axis=1, tiled=True)


def back_product(d_pre, weight):
    return lax.dot_general(
        d_pre, weight, (((1,), (1,)), ((), ())), preferred_element_type=jnp.float32
    )


def mesh_back(d_pre, weight):
    return lax.psum_scatter(
        back_product(d_pre, weight).astype(jnp.bfloat16), "feat", scatter_dimension=1, tiled=True
    ).astype(jnp.float32)


def contract_rows(left_rows, right_rows):
    return lax.dot_general(
        left_rows, right_rows, (((0,), (0,)), ((), ())), preferred_element_type=jnp.float32
    )


def local(grid_in, mesh_in, w_enc, w_proc, w_dec, enc_dst, enc_count, dec_src, proc_src, cotangent):
    n_mesh = lax.axis_size("mesh")
    n_lat = lax.axis_size("lat")
    shard_rows = mesh_in.shape[0]
    home_rows = shard_rows // n_lat
    grid_rows = grid_in.shape[0]
    enc_factor = home_rows / grid_rows
    band_index = lax.axis_index("lat") * n_mesh + lax.axis_index("mesh")
    home_first = lax.axis_index("lat") * home_rows
    win_rows = 3 * home_rows
    enc_valid = jnp.arange(KE, dtype=jnp.int32)[None, :] < enc_count[:, None]
    enc_matrix = window_matrix(
        window_slots(enc_dst, enc_valid, shard_rows, home_rows, n_mesh, band_index), win_rows
    )
    dec_valid = jnp.ones(dec_src.shape, jnp.bool_)
    dec_matrix = window_matrix(
        window_slots(dec_src, dec_valid, shard_rows, home_rows, n_mesh, band_index), win_rows
    )
    grid_full = lax.all_gather(grid_in, "feat", axis=1, tiled=True)
    pre_enc = jnp.dot(grid_full, w_enc, preferred_element_type=jnp.float32)
    enc_msg = jax.nn.silu(pre_enc).astype(jnp.bfloat16)
    enc_window = jnp.dot(enc_matrix, enc_msg, preferred_element_type=jnp.float32) * enc_factor
    aggregate_home = band_sum(enc_window, home_rows)
    mesh_home = lax.dynamic_slice_in_dim(mesh_in, home_first, home_rows, 0)
    latent_one = collect_rows((mesh_home.astype(jnp.float32) + aggregate_home).astype(jnp.bfloat16))
    one_full = widen(latent_one)
    pre_proc = jnp.dot(one_full, w_proc, preferred_element_type=jnp.float32)
    proc_msg = jax.nn.silu(pre_proc).astype(jnp.bfloat16)

    def incidence(row_count):
        node_ids = jnp.arange(row_count, dtype=jnp.int32)
        matrix = jnp.zeros((shard_rows, row_count), jnp.bfloat16)
        for column in range(KP):
            matrix = matrix + (proc_src[:, column][:, None] == node_ids[None, :]).astype(
                jnp.bfloat16
            )
        return matrix

    shard_piece = lax.all_gather(proc_msg, "mesh", axis=0, tiled=True)
    neighbour_sum = jnp.dot(
        incidence(shard_piece.shape[0]), shard_piece, preferred_element_type=jnp.float32
    )
    latent_two = (latent_one.astype(jnp.float32) + neighbour_sum / KP).astype(jnp.bfloat16)
    two_full = widen(latent_two)
    pre_dec = jnp.dot(two_full, w_dec, preferred_element_type=jnp.float32)
    dec_window = jnp.dot(dec_matrix, cotangent, preferred_element_type=jnp.float32) / KD
    d_dec = collect_rows(band_sum(dec_window, home_rows).astype(jnp.bfloat16))
    d_pre_dec = (d_dec.astype(jnp.float32) * silu_grad(pre_dec)).astype(jnp.bfloat16)
    d_two = mesh_back(d_pre_dec, w_dec)
    d_two_b = d_two.astype(jnp.bfloat16)
    d_proc = (
        lax.psum_scatter(
            contract_rows(incidence(shard_rows * lax.axis_size("mesh")), d_two_b).astype(
                jnp.bfloat16
            ),
            "mesh",
            scatter_dimension=0,
            tiled=True,
        ).astype(jnp.float32)
        / KP
    )
    d_pre_proc = (d_proc * silu_grad(pre_proc)).astype(jnp.bfloat16)
    d_one = d_two + mesh_back(d_pre_proc, w_proc)
    grad_mesh = d_one.astype(jnp.bfloat16)
    grad_home = lax.dynamic_slice_in_dim(grad_mesh, home_first, home_rows, 0)
    mesh_window = with_halo(grad_home, ((("lat", "mesh"), 0),), home_rows)
    d_enc = contract_rows(enc_matrix, mesh_window) * enc_factor
    d_pre_enc = (d_enc * silu_grad(pre_enc)).astype(jnp.bfloat16)
    grid_terms = lax.psum_scatter(
        back_product(d_pre_enc, w_enc).astype(jnp.bfloat16), "feat", scatter_dimension=1, tiled=True
    ).astype(jnp.float32)
    grad_grid = (cotangent.astype(jnp.float32) + grid_terms).astype(jnp.bfloat16)
    enc_term = contract_rows(grid_full, d_pre_enc)
    grad_w_proc, grad_w_dec = (
        lax.psum(contract_rows(one_full, d_pre_proc).astype(jnp.bfloat16), "mesh").astype(
            jnp.float32
        ),
        lax.psum(contract_rows(two_full, d_pre_dec).astype(jnp.bfloat16), "mesh").astype(
            jnp.float32
        ),
    )
    grad_w_enc = lax.psum(enc_term, ("lat", "mesh"))
    return (grad_grid, grad_mesh, grad_w_enc, grad_w_proc, grad_w_dec)


def solution(mesh):
    placed = (
        P(("groups", "lat", "mesh"), "feat"),
        P(("groups", "mesh"), "feat"),
        P(None, "feat"),
        P(None, "feat"),
        P(None, "feat"),
        P(("groups", "lat", "mesh"), None),
        P(("groups", "lat", "mesh")),
        P(("groups", "lat", "mesh"), None),
        P(("groups", "mesh"), None),
        P(("groups", "lat", "mesh"), "feat"),
    )
    return jax.shard_map(
        local,
        mesh=mesh,
        in_specs=placed,
        out_specs=(
            P(("groups", "lat", "mesh"), "feat"),
            P(("groups", "mesh"), "feat"),
            P("groups", "feat"),
            P("groups", "feat"),
            P("groups", "feat"),
        ),
        check_vma=False,
    )
```

profile of v0, /device:TPU:0, one launch (start us, length us, event | category | flops | bytes accessed | tf_op | source)
XLA Modules:
  0.0 247.2 jit_solution(12161992677328158249)
XLA Ops:
  8.1 1.4 fusion.10
  9.4 1.4 collective-permute-start.1
  10.9 5.5 %collective-permute-start = (bf16[3,128,256]{2,1,0:T(8,128)(2,1)S(1)}, bf16[3,128,256]{2,1,0:T(8,128)(2,1)S(1)}, u32[]{:S(2)}, u32[]{:S(2)}) collective-permute-start(bf16[3,128,256]{2,1,0:T(8,128)(2,1)S(1)} %bitcast.48), channel_id=1, source_target_pairs={{0,2},{2,4},{4,6},{6,8},{8,10},{10,12},{12,14},{1,3},{3,5},{5,7},{... | collective-permute-start | bytes 589832 | tf_op jit(solution)/shard_map/ppermute | solution.py:18
  16.5 2.2 all_gather.19
  20.8 5.5 %collective-permute-start.2 = (bf16[3,128,256]{2,1,0:T(8,128)(2,1)S(1)}, bf16[3,128,256]{2,1,0:T(8,128)(2,1)S(1)}, u32[]{:S(2)}, u32[]{:S(2)}) collective-permute-start(bf16[3,128,256]{2,1,0:T(8,128)(2,1)S(1)} %bitcast.51), channel_id=1, source_target_pairs={{0,2},{2,4},{4,6},{6,8},{8,10},{10,12},{12,14},{1,3},{3,5},{5,7},{... | collective-permute-start | bytes 589832 | tf_op jit(solution)/shard_map/ppermute | solution.py:18
  26.4 15.0 %all-gather = bf16[1,512,256]{2,1,0:T(8,128)(2,1)S(1)} all-gather(bf16[1,128,256]{2,1,0:T(8,128)(2,1)S(1)} %fusion.51), channel_id=2, replica_groups=mesh['groups'=2,'lat'=4,'mesh'=2,'feat'=2] {'lat'}, dimensions={1}, use_global_device_ids=true | all-gather | bytes 327680 | tf_op jit(solution)/shard_map/all_gather | solution.py:54
  42.2 13.9 %all_gather.20 = bf16[512,256]{1,0:T(8,128)(2,1)S(1)} all-gather(bf16[128,256]{1,0:T(8,128)(2,1)S(1)} %fusion.49), channel_id=1, replica_groups=mesh['groups'=2,'lat'=4,'mesh'=2,'feat'=2] {'lat'}, dimensions={0}, use_global_device_ids=true | all-gather | bytes 327680 | tf_op jit(solution)/shard_map/all_gather | solution.py:54
  56.1 2.2 all_gather.21
  59.4 9.8 %all_gather.22 = bf16[1024,256]{1,0:T(8,128)(2,1)S(1)} all-gather(bf16[512,256]{1,0:T(8,128)(2,1)S(1)} %get-tuple-element.25), channel_id=1, replica_groups=mesh['groups'=2,'lat'=4,'mesh'=2,'feat'=2] {'mesh'}, dimensions={0}, use_global_device_ids=true | all-gather | bytes 786432 | tf_op jit(solution)/shard_map/all_gather | solution.py:117
  69.1 1.8 fusion.9
  70.9 2.3 all_gather.23
  74.9 9.6 %reduce-scatter.5.cloned.1.call-done = bf16[512,256]{1,0:T(8,128)(2,1)} async-done(((bf16[512,512]{1,0:T(8,128)(2,1)}), bf16[512,256]{1,0:T(8,128)(2,1)}) %reduce-scatter.5.cloned.1.call-update) | async-done | bytes 262160 | tf_op jit(solution)/shard_map/reduce_scatter | solution.py:68
  84.6 3.6 %convolution_convert_fusion = bf16[1024,256]{1,0:T(8,128)(2,1)} fusion(bf16[512,256]{1,0:T(8,128)(2,1)} %reduce-scatter.5.cloned.1.call-done, s32[512]{0:T(512)S(1)} %bitcast.62, s32[512]{0:T(512)S(1)} %bitcast.64, s32[512]{0:T(512)S(1)} %bitcast.56, s32[512]{0:T(512)S(1)} %bitcast.58, s32[512]{0:T(512)S(1)} %bitcast.60, s32[512]{0:T(512)S(1)} %bitcast.54), kind=kOutput, calls=%fused_computation.12 | convolution fusion | flops 281280512 | bytes 798720 | tf_op jit(solution)/shard_map/dot_general | solution.py:74
  88.3 15.8 %reduce-scatter.7.cloned.1.call-done = bf16[512,256]{1,0:T(8,128)(2,1)} async-done(((bf16[1024,256]{1,0:T(8,128)(2,1)}), bf16[512,256]{1,0:T(8,128)(2,1)}) %reduce-scatter.7.cloned.1.call-update) | async-done | bytes 262160 | tf_op jit(solution)/shard_map/reduce_scatter | solution.py:130
  104.1 1.3 multiply_convert_fusion
  107.6 7.2 %reduce-scatter.9.cloned.1.call-done = bf16[512,256]{1,0:T(8,128)(2,1)} async-done(((bf16[512,512]{1,0:T(8,128)(2,1)}), bf16[512,256]{1,0:T(8,128)(2,1)}) %reduce-scatter.9.cloned.1.call-update) | async-done | bytes 262160 | tf_op jit(solution)/shard_map/reduce_scatter | solution.py:68
  115.9 1.3 collective-permute-start.5
  117.2 4.5 %collective-permute-start.4 = (bf16[128,256]{1,0:T(8,128)(2,1)S(1)}, bf16[128,256]{1,0:T(8,128)(2,1)S(1)}, u32[]{:S(2)}, u32[]{:S(2)}) collective-permute-start(bf16[128,256]{1,0:T(8,128)(2,1)S(1)} %constant_dynamic-slice_fusion), channel_id=1, source_target_pairs={{0,2},{2,4},{4,6},{6,8},{8,10},{10,12},{12,14},{1,3},{3,5},{5,7},{... | collective-permute-start | bytes 196616 | tf_op jit(solution)/shard_map/ppermute | solution.py:18
  126.6 26.4 %all-reduce.6.cloned.1.call-done = (bf16[512,256]{1,0:T(8,128)(2,1)}, bf16[512,256]{1,0:T(8,128)(2,1)}) async-done(((bf16[512,256]{1,0:T(8,128)(2,1)}, bf16[512,256]{1,0:T(8,128)(2,1)}), (bf16[512,256]{1,0:T(8,128)(2,1)}, bf16[512,256]{1,0:T(8,128)(2,1)})) %all-reduce.6.cloned.1.call-update) | async-done | bytes 524304 | tf_op jit(solution)/shard_map/psum | solution.py:153
  152.9 1.8 convert_element_type.188
  155.6 73.6 %all-reduce.4.cloned.1.call-done = f32[512,256]{0,1:T(8,128)} async-done(((f32[512,256]{0,1:T(8,128)}), f32[512,256]{0,1:T(8,128)}) %all-reduce.4.cloned.1.call-update) | async-done | bytes 524304 | tf_op jit(solution)/shard_map/psum | solution.py:160
  229.2 2.0 copy.15
  231.2 7.4 %reduce-scatter.11.cloned.1.call-done = bf16[512,256]{1,0:T(8,128)(2,1)} async-done(((bf16[512,512]{1,0:T(8,128)(2,1)}), bf16[512,256]{1,0:T(8,128)(2,1)}) %reduce-scatter.11.cloned.1.call-update) | async-done | bytes 262160 | tf_op jit(solution)/shard_map/reduce_scatter | solution.py:147
  238.6 1.7 add_convert_fusion
  (63 shorter events, 15.7 us)
Async XLA Ops:
  7.2 51.1 %copy-start = (bf16[512,256]{1,0:T(8,128)(2,1)S(1)}, bf16[512,256]{1,0:T(8,128)(2,1)}, u32[]{:S(2)}) copy-start(bf16[512,256]{1,0:T(8,128)(2,1)} %param.13) | copy-start | bytes 786436
  7.2 77.4 %reduce-scatter.5.cloned.1.call-start = ((), (), s32[]{:S(2)}) async-start(), calls=%async_computation.4 | async-start | bytes 786432 | tf_op jit(solution)/shard_map/reduce_scatter | solution.py:68
  8.0 8.4 %copy-start.9 = (s32[512,4]{0,1:T(4,128)S(1)}, s32[512,4]{0,1:T(4,128)}, u32[]{:S(2)}) copy-start(s32[512,4]{0,1:T(4,128)} %param.15) | copy-start | bytes 24580
  8.0 8.4 %copy-start.10 = (s32[512]{0:T(512)S(1)}, s32[512]{0:T(512)}, u32[]{:S(2)}) copy-start(s32[512]{0:T(512)} %param.16) | copy-start | bytes 6148
  8.0 8.4 %copy-start.4 = (bf16[512,256]{1,0:T(8,128)(2,1)S(1)}, bf16[512,256]{1,0:T(8,128)(2,1)}, u32[]{:S(2)}) copy-start(bf16[512,256]{1,0:T(8,128)(2,1)} %param.10) | copy-start | bytes 786436
  9.4 9.2 %copy-start.2 = (bf16[512,256]{1,0:T(8,128)(2,1)S(1)}, bf16[512,256]{1,0:T(8,128)(2,1)}, u32[]{:S(2)}) copy-start(bf16[512,256]{1,0:T(8,128)(2,1)} %param.12) | copy-start | bytes 786436
  9.4 16.9 %collective-permute-start.1 = (bf16[3,128,256]{2,1,0:T(8,128)(2,1)S(1)}, bf16[3,128,256]{2,1,0:T(8,128)(2,1)S(1)}, u32[]{:S(2)}, u32[]{:S(2)}) collective-permute-start(bf16[3,128,256]{2,1,0:T(8,128)(2,1)S(1)} %bitcast.47), channel_id=1, source_target_pairs={{2,0},{4,2},{6,4},{8,6},{10,8},{12,10},{14,12},{3,1},{5,3},{7,5},{... | collective-permute-start | bytes 589832 | tf_op jit(solution)/shard_map/ppermute | solution.py:19
  10.9 15.5 %collective-permute-start = (bf16[3,128,256]{2,1,0:T(8,128)(2,1)S(1)}, bf16[3,128,256]{2,1,0:T(8,128)(2,1)S(1)}, u32[]{:S(2)}, u32[]{:S(2)}) collective-permute-start(bf16[3,128,256]{2,1,0:T(8,128)(2,1)S(1)} %bitcast.48), channel_id=1, source_target_pairs={{0,2},{2,4},{4,6},{6,8},{8,10},{10,12},{12,14},{1,3},{3,5},{5,7},{... | collective-permute-start | bytes 589832 | tf_op jit(solution)/shard_map/ppermute | solution.py:18
  19.0 7.3 %copy-start.8 = (s32[512,6]{0,1:T(8,128)S(1)}, s32[512,6]{0,1:T(8,128)}, u32[]{:S(2)}) copy-start(s32[512,6]{0,1:T(8,128)} %param.18) | copy-start | bytes 36868
  19.5 21.8 %collective-permute-start.3 = (bf16[3,128,256]{2,1,0:T(8,128)(2,1)S(1)}, bf16[3,128,256]{2,1,0:T(8,128)(2,1)S(1)}, u32[]{:S(2)}, u32[]{:S(2)}) collective-permute-start(bf16[3,128,256]{2,1,0:T(8,128)(2,1)S(1)} %bitcast.50), channel_id=1, source_target_pairs={{2,0},{4,2},{6,4},{8,6},{10,8},{12,10},{14,12},{3,1},{5,3},{7,5},{... | collective-permute-start | bytes 589832 | tf_op jit(solution)/shard_map/ppermute | solution.py:19
  20.8 20.5 %collective-permute-start.2 = (bf16[3,128,256]{2,1,0:T(8,128)(2,1)S(1)}, bf16[3,128,256]{2,1,0:T(8,128)(2,1)S(1)}, u32[]{:S(2)}, u32[]{:S(2)}) collective-permute-start(bf16[3,128,256]{2,1,0:T(8,128)(2,1)S(1)} %bitcast.51), channel_id=1, source_target_pairs={{0,2},{2,4},{4,6},{6,8},{8,10},{10,12},{12,14},{1,3},{3,5},{5,7},{... | collective-permute-start | bytes 589832 | tf_op jit(solution)/shard_map/ppermute | solution.py:18
  70.9 2.3 copy-start.1
  74.9 29.2 %reduce-scatter.7.cloned.1.call-start = ((), (), s32[]{:S(2)}) async-start(), calls=%async_computation.5 | async-start | bytes 786432 | tf_op jit(solution)/shard_map/reduce_scatter | solution.py:130
  88.2 26.7 %reduce-scatter.9.cloned.1.call-start = ((), (), s32[]{:S(2)}) async-start(), calls=%async_computation.6 | async-start | bytes 786432 | tf_op jit(solution)/shard_map/reduce_scatter | solution.py:68
  106.5 8.3 %copy-start.7 = (bf16[512,256]{1,0:T(8,128)(2,1)S(1)}, bf16[512,256]{1,0:T(8,128)(2,1)}, u32[]{:S(2)}) copy-start(bf16[512,256]{1,0:T(8,128)(2,1)} %reduce-scatter.5.cloned.1.call-done) | copy-start | bytes 786436
  106.5 46.4 %all-reduce.6.cloned.1.call-start = ((), (), s32[]{:S(2)}) async-start(), calls=%async_computation.9 | async-start | bytes 1048576 | tf_op jit(solution)/shard_map/psum | solution.py:153
  115.9 6.9 %copy-start.3 = (bf16[512,256]{1,0:T(8,128)(2,1)}, bf16[512,256]{1,0:T(8,128)(2,1)S(1)}, u32[]{:S(2)}) copy-start(bf16[512,256]{1,0:T(8,128)(2,1)S(1)} %add_convert_fusion.1) | copy-start | bytes 786436
  115.9 7.0 %collective-permute-start.5 = (bf16[128,256]{1,0:T(8,128)(2,1)S(1)}, bf16[128,256]{1,0:T(8,128)(2,1)S(1)}, u32[]{:S(2)}, u32[]{:S(2)}) collective-permute-start(bf16[128,256]{1,0:T(8,128)(2,1)S(1)} %constant_dynamic-slice_fusion), channel_id=1, source_target_pairs={{2,0},{4,2},{6,4},{8,6},{10,8},{12,10},{14,12},{3,1},{5,3},{7,5},{... | collective-permute-start | bytes 196616 | tf_op jit(solution)/shard_map/ppermute | solution.py:19
  117.2 6.4 %collective-permute-start.4 = (bf16[128,256]{1,0:T(8,128)(2,1)S(1)}, bf16[128,256]{1,0:T(8,128)(2,1)S(1)}, u32[]{:S(2)}, u32[]{:S(2)}) collective-permute-start(bf16[128,256]{1,0:T(8,128)(2,1)S(1)} %constant_dynamic-slice_fusion), channel_id=1, source_target_pairs={{0,2},{2,4},{4,6},{6,8},{8,10},{10,12},{12,14},{1,3},{3,5},{5,7},{... | collective-permute-start | bytes 196616 | tf_op jit(solution)/shard_map/ppermute | solution.py:18
  122.9 106.3 %all-reduce.4.cloned.1.call-start = ((), (), s32[]{:S(2)}) async-start(), calls=%async_computation.8 | async-start | bytes 1048576 | tf_op jit(solution)/shard_map/psum | solution.py:160
  125.4 113.3 %reduce-scatter.11.cloned.1.call-start = ((), (), s32[]{:S(2)}) async-start(), calls=%async_computation.7 | async-start | bytes 786432 | tf_op jit(solution)/shard_map/reduce_scatter | solution.py:147
  152.9 1.8 copy-start.6
  155.6 83.0 %copy-start.5 = (bf16[512,256]{1,0:T(8,128)(2,1)S(1)}, bf16[512,256]{1,0:T(8,128)(2,1)}, u32[]{:S(2)}) copy-start(bf16[512,256]{1,0:T(8,128)(2,1)} %param.19) | copy-start | bytes 786436
Sparse Core Ops, SparseCore 0:
  75.0 9.5 reduce-scatter.4
  88.3 15.6 reduce-scatter.6
  106.9 7.9 reduce-scatter.8
  123.0 29.9 all-reduce.5
  156.8 72.3 all-reduce.3
  231.3 7.2 reduce-scatter.10
where the time goes:
time: 248 us; the launch traced here: 247 us
  waiting for transfers between devices  141 us (57%)
  blocking collectives  45.3 us (18%)
  starting transfers between devices  19.7 us (8%)
  matrix products  16.1 us (6%)
  between operations  14.4 us (6%)
  other arithmetic  8.63 us (3%)
    psum x1, waiting for transfers between devices, local(): grad_w_enc = lax.psum(enc_term, ('lat', 'mesh'))  73.6 us
    all_gather x2, blocking collectives, collect_rows(): return lax.all_gather(home_block, 'lat', axis=0, tiled=True)  28.8 us
    psum x1, waiting for transfers between devices, local(): lax.psum(contract_rows(one_full, d_pre_proc).astype(jnp.bfloat16), 'mesh')  26.4 us
    reduce_scatter x2, waiting for transfers between devices, mesh_back(): lax.psum_scatter(back_product(d_pre, weight).astype(jnp.bfloat16), 'feat'...  16.9 us
    reduce_scatter x1, waiting for transfers between devices, local(): lax.psum_scatter(contract_rows(incidence(shard_rows * lax.axis_size('mesh...  15.8 us
    ppermute x3, starting transfers between devices, with_halo(): before = lax.ppermute(last, axis, up)  15.5 us
    all_gather x1, blocking collectives, local(): shard_piece = lax.all_gather(proc_msg, 'mesh', axis=0, tiled=True)  9.76 us
    reduce_scatter x1, waiting for transfers between devices, local(): lax.psum_scatter(back_product(d_pre_enc, w_enc).astype(jnp.bfloat16), 'fe...  7.43 us
  transfers between devices with their start and end apart: 12, of which 7 were waited for; matrix products, arithmetic and copies ran while one was open for 4% of the time, Pallas kernels for 0%

commit v1 on v0

--- a/solution.py
+++ b/solution.py
@@ -1,6 +1,10 @@
+import functools
+
 import jax
 import jax.numpy as jnp
 from jax import lax
+from jax.experimental import pallas as pl
+from jax.experimental.pallas import tpu as pltpu
 from jax.sharding import PartitionSpec as P
 
 KE = 4
@@ -76,7 +80,7 @@
     )
 
 
-def local(grid_in, mesh_in, w_enc, w_proc, w_dec, enc_dst, enc_count, dec_src, proc_src, cotangent):
+def local_staged(grid_in, mesh_in, w_enc, w_proc, w_dec, enc_dst, enc_count, dec_src, proc_src, cotangent):
     n_mesh = lax.axis_size("mesh")
     n_lat = lax.axis_size("lat")
     shard_rows = mesh_in.shape[0]
@@ -161,7 +165,445 @@
     return (grad_grid, grad_mesh, grad_w_enc, grad_w_proc, grad_w_dec)
 
 
+BF = jnp.bfloat16
+F32 = jnp.float32
+NN = (((1,), (0,)), ((), ()))
+NT = (((1,), (1,)), ((), ()))
+TN = (((0,), (0,)), ((), ()))
+
+
+def mm(left, right, dims=NN):
+    return lax.dot_general(left, right, dims, preferred_element_type=F32)
+
+
+def sigm(value):
+    return 1.0 / (1.0 + jnp.exp(-value))
+
+
+def fused_kernel(
+    n_lat, n_mesh,
+    grid_ref, mesh_ref, we_ref, wp_ref, wd_ref, gi_ref, pi_ref, cot_ref,
+    gg_ref, gm_ref, gwe_ref, gwp_ref, gwd_ref,
+    gfull, wef, wpf, wdf, psall, pst, idt, enc_m, enc_t, dec_m, inc_a, inc_t,
+    halo_out, halo_in, own_win, sg_enc, one, ddec, sg_proc, pmsg, two, dpd, dtwo, dtwo_b, dpp,
+    gmesh, dpe, dwin, rs_src, rs_own, rs_in, ag,
+    s_f, r_f, s_p, r_p, s_h, r_h, s_z, r_z, s_x, r_x, s_c, r_c, s_rs, r_rs, s_ag, r_ag,
+):
+    rows, half = grid_ref.shape
+    shard = mesh_ref.shape[0]
+    home = shard // n_lat
+    bands = n_lat * n_mesh
+    nodes = shard * n_mesh
+    wide = 2 * half
+    chunk = wide // bands
+    win = 3 * home
+    factor = home / rows
+    l = lax.axis_index("lat")
+    m = lax.axis_index("mesh")
+    f = lax.axis_index("feat")
+    b = l * n_mesh + m
+    mine = pl.ds(pl.multiple_of(f * half, half), half)
+
+    def remote(source, target, send, recv, **where):
+        return pltpu.make_async_remote_copy(
+            src_ref=source, dst_ref=target, send_sem=send, recv_sem=recv,
+            device_id=where, device_id_type=pl.DeviceIdType.MESH,
+        )
+
+    def band_at(index):
+        return {"lat": index // n_mesh, "mesh": lax.rem(index, n_mesh)}
+
+    barrier = pltpu.get_barrier_semaphore()
+    for d in range(1, bands):
+        pl.semaphore_signal(
+            barrier, inc=1, device_id=band_at(lax.rem(b + d, bands)),
+            device_id_type=pl.DeviceIdType.MESH,
+        )
+    pl.semaphore_signal(
+        barrier, inc=1, device_id={"feat": 1 - f}, device_id_type=pl.DeviceIdType.MESH
+    )
+
+    raw = gi_ref[...]
+    inner = raw & (shard - 1)
+    home_id = (inner >> (home.bit_length() - 1)) * n_mesh + (raw >> (shard.bit_length() - 1))
+    ids = (home_id - b + 1) * home + (inner & (home - 1))
+    row = lax.broadcasted_iota(jnp.int32, raw.shape, 0)
+    ids = jnp.where((row < KE) & (row >= raw[KE:KE + 1, :]), -1, ids)
+    idt[...] = ids.astype(F32).T
+
+    def one_hot(target, first, count):
+        step = 64
+        for r in range(0, win, step):
+            node = lax.broadcasted_iota(jnp.int32, (step, rows), 0) + r
+            acc = jnp.zeros((step, rows), F32)
+            for k in range(first, first + count):
+                acc = acc + jnp.where(node == ids[k:k + 1, :], 1.0, 0.0)
+            target[r:r + step, :] = acc.astype(BF)
+
+    one_hot(dec_m, KE + 1, KD)
+    dec_win = mm(dec_m[...], cot_ref[...]) / KD
+    halo_out[0] = dec_win[2 * home:, :].astype(BF)
+    halo_out[1] = dec_win[:home, :].astype(BF)
+    own_win[0] = dec_win[home:2 * home, :]
+    one_hot(enc_m, 0, KE)
+    gfull[:, mine] = grid_ref[...]
+    wef[:, mine] = we_ref[...]
+    wpf[:, mine] = wp_ref[...]
+    wdf[:, mine] = wd_ref[...]
+    psall[m] = pi_ref[...]
+
+    @pl.when(b == 0)
+    def _():
+        halo_in[0] = jnp.zeros((home, half), BF)
+        halo_in[2] = jnp.zeros((home, half), BF)
+
+    @pl.when(b == bands - 1)
+    def _():
+        halo_in[1] = jnp.zeros((home, half), BF)
+        halo_in[3] = jnp.zeros((home, half), BF)
+
+    pl.semaphore_wait(barrier, bands)
+
+    wides = [
+        remote(s, t.at[:, mine], s_f.at[i], r_f.at[i], feat=1 - f)
+        for i, (s, t) in enumerate(
+            ((grid_ref, gfull), (we_ref, wef), (wp_ref, wpf), (wd_ref, wdf))
+        )
+    ]
+    indices = [
+        remote(pi_ref, psall.at[m], s_p.at[e - 1], r_p.at[e - 1], mesh=lax.rem(m + e, n_mesh))
+        for e in range(1, n_mesh)
+    ]
+    wides[0].start()
+
+    def halo(i, up):
+        slot = 2 * i + (0 if up else 1)
+        return remote(
+            halo_out.at[slot], halo_in.at[slot], s_h.at[slot], r_h.at[slot],
+            **band_at(b + 1 if up else b - 1),
+        )
+
+    def halo_start(i):
+        @pl.when(b < bands - 1)
+        def _():
+            halo(i, True).start()
+
+        @pl.when(b > 0)
+        def _():
+            halo(i, False).start()
+
+    def halo_recv(i):
+        @pl.when(b > 0)
+        def _():
+            halo(i, True).wait_recv()
+
+        @pl.when(b < bands - 1)
+        def _():
+            halo(i, False).wait_recv()
+
+    def halo_sent(i):
+        @pl.when(b < bands - 1)
+        def _():
+            halo(i, True).wait_send()
+
+        @pl.when(b > 0)
+        def _():
+            halo(i, False).wait_send()
+
+    halo_start(0)
+    for copy in indices + wides[1:]:
+        copy.start()
+
+    wides[0].wait_recv()
+    pre = mm(gfull[...], we_ref[...])
+    enc_win = mm(enc_m[...], (pre * sigm(pre)).astype(BF)) * factor
+    halo_out[2] = enc_win[2 * home:, :].astype(BF)
+    halo_out[3] = enc_win[:home, :].astype(BF)
+    own_win[1] = enc_win[home:2 * home, :]
+    halo_start(1)
+
+    for copy in indices:
+        copy.wait_recv()
+    step = 64
+    for i in range(n_mesh):
+        pst[i * shard:(i + 1) * shard, :] = psall[i].astype(F32).T
+
+    def build_a(t, carry):
+        r = pl.multiple_of(t * step, step)
+        node = lax.broadcasted_iota(jnp.int32, (step, nodes), 1).astype(F32)
+        acc = jnp.zeros((step, nodes), F32)
+        for k in range(KP):
+            acc = acc + jnp.where(node == pst[pl.ds(r, step), k:k + 1], 1.0, 0.0)
+        inc_a[pl.ds(r, step), :] = acc.astype(BF)
+        return carry
+
+    def build_t(t, carry):
+        r = pl.multiple_of(t * step, step)
+        for i in range(n_mesh):
+            node = lax.broadcasted_iota(jnp.int32, (step, shard), 0) + r
+            acc = jnp.zeros((step, shard), F32)
+            for k in range(KP):
+                acc = acc + jnp.where(node == psall[i, k:k + 1, :], 1.0, 0.0)
+            inc_t[pl.ds(r, step), i * shard:(i + 1) * shard] = acc.astype(BF)
+        return carry
+
+    def build_e(t, carry):
+        r = pl.multiple_of(t * step, step)
+        node = lax.broadcasted_iota(jnp.int32, (step, win), 1).astype(F32)
+        acc = jnp.zeros((step, win), F32)
+        for k in range(KE):
+            acc = acc + jnp.where(node == idt[pl.ds(r, step), k:k + 1], 1.0, 0.0)
+        enc_t[pl.ds(r, step), :] = acc.astype(BF)
+        return carry
+
+    def block(array, d, e):
+        at_l = lax.rem(l + n_lat - d, n_lat)
+        at_m = lax.rem(m + n_mesh - e, n_mesh)
+        return array.at[pl.ds(pl.multiple_of(at_m * shard + at_l * home, home), home), mine]
+
+    def along_lat(array, a, d):
+        own = block(array, 0, 0)
+        return remote(own, own, s_z.at[a, d - 1], r_z.at[a, d - 1], lat=lax.rem(l + d, n_lat))
+
+    def recv_lat(array, a, d):
+        view = block(array, d, 0)
+        return remote(view, view, s_z.at[a, d - 1], r_z.at[a, d - 1], lat=lax.rem(l + d, n_lat))
+
+    def along_mesh(array, a, d, e):
+        view = block(array, d, 0)
+        return remote(
+            view, view, s_x.at[a, d, e - 1], r_x.at[a, d, e - 1], mesh=lax.rem(m + e, n_mesh)
+        )
+
+    def recv_mesh(array, a, d, e):
+        view = block(array, d, e)
+        return remote(
+            view, view, s_x.at[a, d, e - 1], r_x.at[a, d, e - 1], mesh=lax.rem(m + e, n_mesh)
+        )
+
+    def along_feat(array, a, d, e):
+        view = block(array, d, e)
+        return remote(view, view, s_c.at[a, d, e], r_c.at[a, d, e], feat=1 - f)
+
+    def spread_own(array, a):
+        for e in range(1, n_mesh):
+            along_mesh(array, a, 0, e).start()
+        for d in range(1, n_lat):
+            along_lat(array, a, d).start()
+        along_feat(array, a, 0, 0).start()
+
+    def spread_lat(array, a):
+        for d in range(1, n_lat):
+            recv_lat(array, a, d).wait_recv()
+            for e in range(1, n_mesh):
+                along_mesh(array, a, d, e).start()
+            along_feat(array, a, d, 0).start()
+
+    def spread_mesh(array, a):
+        for d in range(n_lat):
+            for e in range(1, n_mesh):
+                recv_mesh(array, a, d, e).wait_recv()
+                along_feat(array, a, d, e).start()
+
+    def spread_done(array, a):
+        for d in range(n_lat):
+            for e in range(n_mesh):
+                along_feat(array, a, d, e).wait_recv()
+
+    def spread_sent(array, a):
+        for d in range(1, n_lat):
+            along_lat(array, a, d).wait_send()
+        for d in range(n_lat):
+            for e in range(n_mesh):
+                if e:
+                    along_mesh(array, a, d, e).wait_send()
+                along_feat(array, a, d, e).wait_send()
+
+    def banded(i):
+        return own_win[i] + halo_in[2 * i].astype(F32) + halo_in[2 * i + 1].astype(F32)
+
+    home_rows = pl.ds(pl.multiple_of(m * shard + l * home, home), home)
+    halo_recv(0)
+    ddec[home_rows, mine] = banded(0).astype(BF)
+    halo_recv(1)
+    mesh_home = mesh_ref[pl.ds(pl.multiple_of(l * home, home), home), :].astype(F32)
+    one[home_rows, mine] = (mesh_home + banded(1)).astype(BF)
+    spread_own(one, 0)
+    lax.fori_loop(0, nodes // step, build_a, 0)
+    spread_lat(one, 0)
+    spread_own(ddec, 1)
+    spread_mesh(one, 0)
+    lax.fori_loop(0, nodes // step, build_t, 0)
+    spread_lat(ddec, 1)
+    wides[1].wait_recv()
+    wides[2].wait_recv()
+    wides[3].wait_recv()
+    tile = min(512, nodes)
+    spread_done(one, 0)
+
+    def tiles(body):
+        for r in range(0, nodes, tile):
+            body(slice(r, r + tile))
+
+    def proc(at):
+        value = mm(one[at, :], wpf[...])
+        sig = sigm(value)
+        pmsg[at, :] = (value * sig).astype(BF)
+        sg_proc[at, :] = sig * (1.0 + value * (1.0 - sig))
+
+    tiles(proc)
+    spread_mesh(ddec, 1)
+
+    def second(at):
+        total = mm(inc_a[at, :], pmsg[...])
+        two[at, :] = (one[at, :].astype(F32) + total * (1.0 / KP)).astype(BF)
+
+    tiles(second)
+
+    pre_all = mm(gfull[...], wef[...])
+    sig_all = sigm(pre_all)
+    sg_enc[...] = sig_all * (1.0 + pre_all * (1.0 - sig_all))
+    lax.fori_loop(0, rows // step, build_e, 0)
+    spread_done(ddec, 1)
+
+    def decode(at):
+        value = mm(two[at, :], wdf[...])
+        sig = sigm(value)
+        grad = sig * (1.0 + value * (1.0 - sig))
+        dpd[at, :] = (ddec[at, :].astype(F32) * grad).astype(BF)
+        back = mm(dpd[at, :], wdf[...], NT)
+        dtwo[at, :] = back
+        dtwo_b[at, :] = back.astype(BF)
+
+    tiles(decode)
+
+    def third(at):
+        total = mm(inc_t[at, :], dtwo_b[...]) * (1.0 / KP)
+        dpp[at, :] = (total * sg_proc[at, :]).astype(BF)
+        gmesh[at, :] = (dtwo[at, :] + mm(dpp[at, :], wpf[...], NT)).astype(BF)
+
+    tiles(third)
+
+    for j in range(3):
+        at = jnp.clip(b + j - 1, 0, bands - 1)
+        first = pl.multiple_of(lax.rem(at, n_mesh) * shard + at // n_mesh * home, home)
+        dwin[j * home:(j + 1) * home, :] = gmesh[pl.ds(first, home), :]
+    dpe[...] = (mm(enc_t[...], dwin[...]) * factor * sg_enc[...]).astype(BF)
+    weight = mm(gfull[...], dpe[:, mine], TN)
+    rs_own[...] = weight
+    rs_src[...] = weight.astype(BF)
+
+    def part(index):
+        return pl.ds(pl.multiple_of(index * chunk, chunk), chunk)
+
+    scatter, gather = [], []
+    for d in range(1, bands):
+        to = lax.rem(b + d, bands)
+        scatter.append(
+            remote(
+                rs_src.at[part(to), :], rs_in.at[d - 1], s_rs.at[d - 1], r_rs.at[d - 1],
+                **band_at(to),
+            )
+        )
+        scatter[-1].start()
+    gwd_ref[...] = mm(two[...], dpd[:, mine], TN)
+    gwp_ref[...] = mm(one[...], dpp[:, mine], TN)
+    total = rs_own[part(b), :]
+    for d in range(1, bands):
+        scatter[d - 1].wait_recv()
+        total = total + rs_in[d - 1].astype(F32)
+    ag[part(b), :] = total.astype(BF)
+    for d in range(1, bands):
+        gather.append(
+            remote(
+                ag.at[part(b), :], ag.at[part(b), :], s_ag.at[d - 1], r_ag.at[d - 1],
+                **band_at(lax.rem(b + d, bands)),
+            )
+        )
+        gather[-1].start()
+    terms = mm(dpe[...], wef[mine, :], NT)
+    gg_ref[...] = (cot_ref[...].astype(F32) + terms).astype(BF)
+    gm_ref[...] = gmesh[pl.ds(pl.multiple_of(m * shard, shard), shard), mine]
+    for copy in wides + indices:
+        copy.wait_send()
+    halo_sent(0)
+    halo_sent(1)
+    spread_sent(one, 0)
+    spread_sent(ddec, 1)
+    for copy in scatter:
+        copy.wait_send()
+    for d in range(1, bands):
+        view = ag.at[part(lax.rem(b + bands - d, bands)), :]
+        remote(
+            view, view, s_ag.at[d - 1], r_ag.at[d - 1], **band_at(lax.rem(b + d, bands))
+        ).wait_recv()
+    gwe_ref[...] = ag[...].astype(F32)
+    for copy in gather:
+        copy.wait_send()
+
+
+def local_fused(
+    grid_in, mesh_in, w_enc, w_proc, w_dec, enc_dst, enc_count, dec_src, proc_src, cotangent
+):
+    n_mesh = lax.axis_size("mesh")
+    n_lat = lax.axis_size("lat")
+    rows, half = grid_in.shape
+    shard = mesh_in.shape[0]
+    wide = 2 * half
+    home = shard // n_lat
+    bands = n_lat * n_mesh
+    nodes = shard * n_mesh
+    win = 3 * home
+    grid_index = jnp.concatenate([enc_dst.T, enc_count[None, :], dec_src.T], axis=0)
+    node_index = jnp.pad(proc_src.T, ((0, 8 - KP), (0, 0)))
+    v = pltpu.VMEM
+    dma = pltpu.SemaphoreType.DMA
+    vmem = pl.BlockSpec(memory_space=pltpu.VMEM)
+    shaped = jax.ShapeDtypeStruct
+    return tuple(pl.pallas_call(
+        functools.partial(fused_kernel, n_lat, n_mesh),
+        out_shape=(
+            shaped((rows, half), BF),
+            shaped((shard, half), BF),
+            shaped((wide, half), F32),
+            shaped((wide, half), F32),
+            shaped((wide, half), F32),
+        ),
+        in_specs=[vmem] * 8,
+        out_specs=(vmem,) * 5,
+        scratch_shapes=[
+            v((rows, wide), BF), v((wide, wide), BF), v((wide, wide), BF), v((wide, wide), BF),
+            v((n_mesh, 8, shard), jnp.int32), v((nodes, 8), F32), v((rows, 8), F32),
+            v((win, rows), BF), v((rows, win), BF), v((win, rows), BF),
+            v((nodes, nodes), BF), v((nodes, nodes), BF),
+            v((4, home, half), BF), v((4, home, half), BF), v((2, home, half), F32),
+            v((rows, wide), F32),
+            v((nodes, wide), BF), v((nodes, wide), BF), v((nodes, wide), F32),
+            v((nodes, wide), BF), v((nodes, wide), BF), v((nodes, wide), BF),
+            v((nodes, wide), F32), v((nodes, wide), BF), v((nodes, wide), BF),
+            v((nodes, wide), BF), v((rows, wide), BF), v((win, wide), BF),
+            v((wide, half), BF), v((wide, half), F32),
+            v((bands - 1, wide // bands, half), BF), v((wide, half), BF),
+            dma((4,)), dma((4,)), dma((n_mesh - 1,)), dma((n_mesh - 1,)),
+            dma((4,)), dma((4,)),
+            dma((2, n_lat - 1)), dma((2, n_lat - 1)),
+            dma((2, n_lat, n_mesh - 1)), dma((2, n_lat, n_mesh - 1)),
+            dma((2, n_lat, n_mesh)), dma((2, n_lat, n_mesh)),
+            dma((bands - 1,)), dma((bands - 1,)), dma((bands - 1,)), dma((bands - 1,)),
+        ],
+        compiler_params=pltpu.CompilerParams(
+            collective_id=0, has_side_effects=True, vmem_limit_bytes=56 * 1024 * 1024
+        ),
+        cost_estimate=pl.CostEstimate(
+            flops=10 * nodes * wide * wide, bytes_accessed=8 * rows * wide,
+            transcendentals=4 * nodes * wide,
+        ),
+    )(grid_in, mesh_in, w_enc, w_proc, w_dec, grid_index, node_index, cotangent))
+
+
 def solution(mesh):
+    bands = mesh.shape["lat"] * mesh.shape["mesh"]
+    body = local_fused if bands <= 8 and mesh.shape["feat"] == 2 else local_staged
     placed = (
         P(("groups", "lat", "mesh"), "feat"),
         P(("groups", "mesh"), "feat"),
@@ -175,7 +617,7 @@
         P(("groups", "lat", "mesh"), "feat"),
     )
     return jax.shard_map(
-        local,
+        body,
         mesh=mesh,
         in_specs=placed,
         out_specs=(

time: 248 us -> 64.3 us (0.26)
  waiting for transfers between devices: 141 us -> 0 us
  Pallas kernels: 0 us -> 54.9 us
  blocking collectives: 45.3 us -> 0 us
  starting transfers between devices: 19.7 us -> 0 us
  matrix products: 16.1 us -> 0 us
  between operations: 14.4 us -> 0.67 us
  other arithmetic: 8.63 us -> 1.34 us
  local copies, waits for them, and re-layouts: 2.14 us -> 6.99 us
    psum x2 -> x0, waiting for transfers between devices: 99.9 us -> none  [the longest x1 73.6 us: local(): grad_w_enc = lax.psum(enc_term, ('lat', 'mesh'))]
    pallas_call x0 -> x1, Pallas kernels: none -> 54.9 us  [local_fused(): pl.pallas_call(functools.partial(fused_kernel, n_lat, n_mesh), out_shape=...]
    all_gather x6 -> x0, blocking collectives: 45.3 us -> none  [the longest x2 28.8 us: collect_rows(): return lax.all_gather(home_block, 'lat', axis=0, tiled=True)]
    reduce_scatter x4 -> x0, waiting for transfers between devices: 40.1 us -> none  [the longest x2 16.9 us: mesh_back(): lax.psum_scatter(back_product(d_pre, weight).astype(jnp.bfloat16), 'feat'...]
    ppermute x6 -> x0, starting transfers between devices: 19.5 us -> none  [the longest x3 15.5 us: with_halo(): before = lax.ppermute(last, axis, up)]
    dot_general x14 -> x0, matrix products: 16.1 us -> none  [the longest x5 7.38 us: contract_rows(): lax.dot_general(left_rows, right_rows, (((0,), (0,)), ((), ())), preferre...]
    convert_element_type x8 -> x0, other arithmetic: 7.82 us -> none  [the longest x1 1.82 us: local(): lax.psum(contract_rows(one_full, d_pre_proc).astype(jnp.bfloat16), 'mesh')]
    unnamed x23 -> x17, local copies, waits for them, and re-layouts: 2.1 us -> 6.38 us
  transfers between devices with their start and end apart: 12 -> 0, of which waited for: 7 -> 0; matrix products, arithmetic and copies ran while one was open for 4% -> 0% of each run, Pallas kernels for 0% -> 0%
where the time goes in v1:
time: 64.3 us; the launch traced here: 63.9 us
  Pallas kernels  54.9 us (85%)
  local copies, waits for them, and re-layouts  6.99 us (11%)
  other arithmetic  1.34 us (2%)
  between operations  0.67 us (1%)
    pallas_call x1, Pallas kernels, local_fused(): pl.pallas_call(functools.partial(fused_kernel, n_lat, n_mesh), out_shape=...  54.9 us
    unnamed x17, local copies, waits for them, and re-layouts  6.38 us
    concatenate x1, other arithmetic, local_fused(): jnp.concatenate([enc_dst.T, enc_count[None, :], dec_src.T], axis=0)  1.34 us

profile of v1, /device:TPU:0, one launch (start us, length us, event | category | flops | bytes accessed | tf_op | source)
XLA Modules:
  0.0 63.9 jit_solution(10803140159478675551)
XLA Ops:
  0.6 0.0 copy-start.5
  0.6 0.7 %copy-done.5 = s32[512]{0:T(512)S(1)} copy-done((s32[512]{0:T(512)S(1)}, s32[512]{0:T(512)}, u32[]{:S(2)}) %copy-start.5) | copy-done | bytes 2072
  1.3 0.0 copy-start.4
  1.3 1.3 %pad_add_fusion.gi_ref = s32[8,512]{1,0:T(8,128)} fusion(s32[3,512]{1,0:T(4,128)} %bitcast.5, s32[1,512]{1,0:T(1,128)S(1)} %bitcast.7, s32[4,512]{1,0:T(4,128)} %bitcast.6), kind=kLoop, calls=%fused_computation | loop fusion | flops 8192 | bytes 32768 | tf_op jit(solution)/shard_map/concatenate | solution.py:557
  2.7 0.0 copy-done.4
  2.7 0.6 pad.4.pi_ref
  3.3 54.9 %shard_map.137 = (bf16[512,256]{1,0:T(8,128)(2,1)}, bf16[512,256]{1,0:T(8,128)(2,1)}, f32[512,256]{1,0:T(8,128)}, f32[512,256]{1,0:T(8,128)}, f32[512,256]{1,0:T(8,128)}) custom-call(bf16[512,256]{1,0:T(8,128)(2,1)} %grid_ref.1, bf16[512,256]{1,0:T(8,128)(2,1)} %mesh_ref.1, bf16[512,256]{1,0:T(8,128)(2,1)} %we_ref.1, bf16[512,256]{1,0:T(8,128)(2,1)} %wp_ref.1, ...), custom_call_target="tpu_custom_call" | custom-call | flops 2684354560 | bytes 2097152 | tf_op jit(solution)/shard_map/pallas_call | solution.py:563
  58.2 0.0 copy-start.3
  58.2 0.0 copy-start.2
  58.2 1.7 %copy.20 = bf16[512,256]{1,0:T(8,128)(2,1)} copy(bf16[512,256]{1,0:T(8,128)(2,1)} %get-tuple-element.10) | data formatting | bytes 524288
  59.9 0.0 copy-done.3
  59.9 0.7 %copy.21 = bf16[512,256]{1,0:T(8,128)(2,1)} copy(bf16[512,256]{1,0:T(8,128)(2,1)S(1)} %copy-done.3) | data formatting | bytes 524288
  60.6 0.0 copy-done.2
  60.6 0.0 copy-start.1
  60.6 0.8 %copy.22 = f32[512,256]{1,0:T(8,128)} copy(f32[512,256]{1,0:T(8,128)S(1)} %copy-done.2) | data formatting | bytes 1048576
  61.4 0.4 copy-done.1
  61.9 0.0 copy-start
  61.9 0.8 %copy.23 = f32[512,256]{1,0:T(8,128)} copy(f32[512,256]{1,0:T(8,128)S(1)} %copy-done.1) | data formatting | bytes 1048576
  62.7 0.4 copy-done
  63.1 0.8 %copy.24 = f32[512,256]{1,0:T(8,128)} copy(f32[512,256]{1,0:T(8,128)S(1)} %copy-done) | data formatting | bytes 1048576
Async XLA Ops:
  0.6 0.7 %copy-start.5 = (s32[512]{0:T(512)S(1)}, s32[512]{0:T(512)}, u32[]{:S(2)}) copy-start(s32[512]{0:T(512)} %param.16) | copy-start | bytes 6148
  1.3 1.3 %copy-start.4 = (s32[512,6]{0,1:T(8,128)S(1)}, s32[512,6]{0,1:T(8,128)}, u32[]{:S(2)}) copy-start(s32[512,6]{0,1:T(8,128)} %param.18) | copy-start | bytes 36868
  58.2 1.8 %copy-start.3 = (bf16[512,256]{1,0:T(8,128)(2,1)S(1)}, bf16[512,256]{1,0:T(8,128)(2,1)}, u32[]{:S(2)}) copy-start(bf16[512,256]{1,0:T(8,128)(2,1)} %get-tuple-element.11) | copy-start | bytes 786436
  58.2 2.5 %copy-start.2 = (f32[512,256]{1,0:T(8,128)S(1)}, f32[512,256]{1,0:T(8,128)}, u32[]{:S(2)}) copy-start(f32[512,256]{1,0:T(8,128)} %get-tuple-element.12) | copy-start | bytes 1572868
  60.6 1.2 %copy-start.1 = (f32[512,256]{1,0:T(8,128)S(1)}, f32[512,256]{1,0:T(8,128)}, u32[]{:S(2)}) copy-start(f32[512,256]{1,0:T(8,128)} %get-tuple-element.13) | copy-start | bytes 1572868
  61.9 1.2 %copy-start = (f32[512,256]{1,0:T(8,128)S(1)}, f32[512,256]{1,0:T(8,128)}, u32[]{:S(2)}) copy-start(f32[512,256]{1,0:T(8,128)} %get-tuple-element.14) | copy-start | bytes 1572868

commit v2 on v1

--- a/solution.py
+++ b/solution.py
@@ -182,9 +182,9 @@
 
 def fused_kernel(
     n_lat, n_mesh,
-    grid_ref, mesh_ref, we_ref, wp_ref, wd_ref, gi_ref, pi_ref, cot_ref,
+    grid_ref, mesh_ref, we_ref, wp_ref, wd_ref, dst_ref, count_ref, src_ref, pi_ref, cot_ref,
     gg_ref, gm_ref, gwe_ref, gwp_ref, gwd_ref,
-    gfull, wef, wpf, wdf, psall, pst, idt, enc_m, enc_t, dec_m, inc_a, inc_t,
+    gfull, wef, wpf, wdf, stage, psall, pst, idt, enc_m, enc_t, dec_m, inc_a, inc_t,
     halo_out, halo_in, own_win, sg_enc, one, ddec, sg_proc, pmsg, two, dpd, dtwo, dtwo_b, dpp,
     gmesh, dpe, dwin, rs_src, rs_own, rs_in, ag,
     s_f, r_f, s_p, r_p, s_h, r_h, s_z, r_z, s_x, r_x, s_c, r_c, s_rs, r_rs, s_ag, r_ag,
@@ -223,34 +223,38 @@
         barrier, inc=1, device_id={"feat": 1 - f}, device_id_type=pl.DeviceIdType.MESH
     )
 
-    raw = gi_ref[...]
-    inner = raw & (shard - 1)
-    home_id = (inner >> (home.bit_length() - 1)) * n_mesh + (raw >> (shard.bit_length() - 1))
-    ids = (home_id - b + 1) * home + (inner & (home - 1))
-    row = lax.broadcasted_iota(jnp.int32, raw.shape, 0)
-    ids = jnp.where((row < KE) & (row >= raw[KE:KE + 1, :]), -1, ids)
-    idt[...] = ids.astype(F32).T
-
-    def one_hot(target, first, count):
+    def slots(raw):
+        inner = raw & (shard - 1)
+        home_id = (inner >> (home.bit_length() - 1)) * n_mesh + (raw >> (shard.bit_length() - 1))
+        return (home_id - b + 1) * home + (inner & (home - 1))
+
+    order = lax.broadcasted_iota(jnp.int32, dst_ref.shape, 0)
+    enc_ids = jnp.where(order < count_ref[...], slots(dst_ref[...]), -1)
+    dec_ids = slots(src_ref[...])
+    idt[...] = jnp.concatenate([enc_ids, enc_ids], axis=0).astype(F32).T
+    stage[0:KP, :] = pi_ref[...]
+    stage[KP:8, :] = jnp.zeros((8 - KP, shard), jnp.int32)
+
+    def one_hot(target, ids):
         step = 64
         for r in range(0, win, step):
             node = lax.broadcasted_iota(jnp.int32, (step, rows), 0) + r
             acc = jnp.zeros((step, rows), F32)
-            for k in range(first, first + count):
+            for k in range(ids.shape[0]):
                 acc = acc + jnp.where(node == ids[k:k + 1, :], 1.0, 0.0)
             target[r:r + step, :] = acc.astype(BF)
 
-    one_hot(dec_m, KE + 1, KD)
+    one_hot(dec_m, dec_ids)
     dec_win = mm(dec_m[...], cot_ref[...]) / KD
     halo_out[0] = dec_win[2 * home:, :].astype(BF)
     halo_out[1] = dec_win[:home, :].astype(BF)
     own_win[0] = dec_win[home:2 * home, :]
-    one_hot(enc_m, 0, KE)
+    one_hot(enc_m, enc_ids)
     gfull[:, mine] = grid_ref[...]
     wef[:, mine] = we_ref[...]
     wpf[:, mine] = wp_ref[...]
     wdf[:, mine] = wd_ref[...]
-    psall[m] = pi_ref[...]
+    psall[m] = stage[...]
 
     @pl.when(b == 0)
     def _():
@@ -271,7 +275,7 @@
         )
     ]
     indices = [
-        remote(pi_ref, psall.at[m], s_p.at[e - 1], r_p.at[e - 1], mesh=lax.rem(m + e, n_mesh))
+        remote(stage, psall.at[m], s_p.at[e - 1], r_p.at[e - 1], mesh=lax.rem(m + e, n_mesh))
         for e in range(1, n_mesh)
     ]
     wides[0].start()
@@ -506,8 +510,8 @@
             )
         )
         scatter[-1].start()
-    gwd_ref[...] = mm(two[...], dpd[:, mine], TN)
-    gwp_ref[...] = mm(one[...], dpp[:, mine], TN)
+    gwd_ref[...] = mm(two[...], dpd[:, mine], TN).astype(BF)
+    gwp_ref[...] = mm(one[...], dpp[:, mine], TN).astype(BF)
     total = rs_own[part(b), :]
     for d in range(1, bands):
         scatter[d - 1].wait_recv()
@@ -537,9 +541,14 @@
         remote(
             view, view, s_ag.at[d - 1], r_ag.at[d - 1], **band_at(lax.rem(b + d, bands))
         ).wait_recv()
-    gwe_ref[...] = ag[...].astype(F32)
+    gwe_ref[...] = ag[...]
     for copy in gather:
         copy.wait_send()
+
+
+def widen_kernel(*refs):
+    for source, target in zip(refs[:5], refs[5:]):
+        target[...] = source[...].astype(target.dtype)
 
 
 def local_fused(
@@ -554,26 +563,24 @@
     bands = n_lat * n_mesh
     nodes = shard * n_mesh
     win = 3 * home
-    grid_index = jnp.concatenate([enc_dst.T, enc_count[None, :], dec_src.T], axis=0)
-    node_index = jnp.pad(proc_src.T, ((0, 8 - KP), (0, 0)))
     v = pltpu.VMEM
     dma = pltpu.SemaphoreType.DMA
     vmem = pl.BlockSpec(memory_space=pltpu.VMEM)
     shaped = jax.ShapeDtypeStruct
-    return tuple(pl.pallas_call(
+    parts = pl.pallas_call(
         functools.partial(fused_kernel, n_lat, n_mesh),
         out_shape=(
             shaped((rows, half), BF),
             shaped((shard, half), BF),
-            shaped((wide, half), F32),
-            shaped((wide, half), F32),
-            shaped((wide, half), F32),
+            shaped((wide, half), BF),
+            shaped((wide, half), BF),
+            shaped((wide, half), BF),
         ),
-        in_specs=[vmem] * 8,
+        in_specs=[vmem] * 10,
         out_specs=(vmem,) * 5,
         scratch_shapes=[
             v((rows, wide), BF), v((wide, wide), BF), v((wide, wide), BF), v((wide, wide), BF),
-            v((n_mesh, 8, shard), jnp.int32), v((nodes, 8), F32), v((rows, 8), F32),
+            v((8, shard), jnp.int32), v((n_mesh, 8, shard), jnp.int32), v((nodes, 8), F32), v((rows, 8), F32),
             v((win, rows), BF), v((rows, win), BF), v((win, rows), BF),
             v((nodes, nodes), BF), v((nodes, nodes), BF),
             v((4, home, half), BF), v((4, home, half), BF), v((2, home, half), F32),
@@ -598,7 +605,20 @@
             flops=10 * nodes * wide * wide, bytes_accessed=8 * rows * wide,
             transcendentals=4 * nodes * wide,
         ),
-    )(grid_in, mesh_in, w_enc, w_proc, w_dec, grid_index, node_index, cotangent))
+    )(grid_in, mesh_in, w_enc, w_proc, w_dec, enc_dst.T, enc_count[None, :], dec_src.T, proc_src.T, cotangent)
+    return tuple(pl.pallas_call(
+        widen_kernel,
+        out_shape=(
+            shaped((rows, half), BF),
+            shaped((shard, half), BF),
+            shaped((wide, half), F32),
+            shaped((wide, half), F32),
+            shaped((wide, half), F32),
+        ),
+        in_specs=[vmem] * 5,
+        out_specs=(vmem,) * 5,
+        compiler_params=pltpu.CompilerParams(vmem_limit_bytes=16 * 1024 * 1024),
+    )(*parts))
 
 
 def solution(mesh):

time: 64.3 us -> 61.8 us (0.961)
  local copies, waits for them, and re-layouts: 6.99 us -> 4.74 us
  other arithmetic: 1.34 us -> 0 us
  Pallas kernels: 54.9 us -> 56.1 us
    unnamed x17 -> x10, local copies, waits for them, and re-layouts: 6.38 us -> 4.74 us
    pallas_call x0 -> x1, Pallas kernels: none -> 1.42 us  [local_fused(): pl.pallas_call(widen_kernel, out_shape=(shaped((rows, half), BF), shaped(...]
    concatenate x1 -> x0, other arithmetic: 1.34 us -> none  [local_fused(): jnp.concatenate([enc_dst.T, enc_count[None, :], dec_src.T], axis=0)]
where the time goes in v2:
time: 61.8 us; the launch traced here: 61.5 us
  Pallas kernels  56.1 us (91%)
  local copies, waits for them, and re-layouts  4.74 us (8%)
  between operations  0.66 us (1%)
    pallas_call x1, Pallas kernels, local_fused(): pl.pallas_call(functools.partial(fused_kernel, n_lat, n_mesh), out_shape=...  54.7 us
    unnamed x10, local copies, waits for them, and re-layouts  4.74 us
    pallas_call x1, Pallas kernels, local_fused(): pl.pallas_call(widen_kernel, out_shape=(shaped((rows, half), BF), shaped(...  1.42 us

profile of v2, /device:TPU:0, one launch (start us, length us, event | category | flops | bytes accessed | tf_op | source)
XLA Modules:
  0.0 61.5 jit_solution(7624063926618169273)
XLA Ops:
  0.6 54.7 %shard_map.137 = (bf16[512,256]{1,0:T(8,128)(2,1)}, bf16[512,256]{1,0:T(8,128)(2,1)}, bf16[512,256]{1,0:T(8,128)(2,1)}, bf16[512,256]{1,0:T(8,128)(2,1)}, bf16[512,256]{1,0:T(8,128)(2,1)}) custom-call(bf16[512,256]{1,0:T(8,128)(2,1)} %grid_ref.1, bf16[512,256]{1,0:T(8,128)(2,1)} %mesh_ref.1, bf16[512,256]{1,0:T(8,128)(2,1)} %we_ref.1, ...), custom_call_target="tpu_custom_call" | custom-call | flops 2684354560 | bytes 2097152 | tf_op jit(solution)/shard_map/pallas_call | solution.py:570
  55.3 0.0 copy-start
  55.3 0.9 %copy-done = bf16[512,256]{1,0:T(8,128)(2,1)S(1)} copy-done((bf16[512,256]{1,0:T(8,128)(2,1)S(1)}, bf16[512,256]{1,0:T(8,128)(2,1)}, u32[]{:S(2)}) %copy-start) | copy-done | bytes 262168
  56.3 0.0 copy-start.1
  56.3 0.9 %copy-done.1 = bf16[512,256]{1,0:T(8,128)(2,1)S(1)} copy-done((bf16[512,256]{1,0:T(8,128)(2,1)S(1)}, bf16[512,256]{1,0:T(8,128)(2,1)}, u32[]{:S(2)}) %copy-start.1) | copy-done | bytes 262168
  57.2 0.0 copy-start.2
  57.2 0.9 %copy-done.2 = bf16[512,256]{1,0:T(8,128)(2,1)S(1)} copy-done((bf16[512,256]{1,0:T(8,128)(2,1)S(1)}, bf16[512,256]{1,0:T(8,128)(2,1)}, u32[]{:S(2)}) %copy-start.2) | copy-done | bytes 262168
  58.2 0.0 copy-start.3
  58.2 0.9 %copy-done.3 = bf16[512,256]{1,0:T(8,128)(2,1)S(1)} copy-done((bf16[512,256]{1,0:T(8,128)(2,1)S(1)}, bf16[512,256]{1,0:T(8,128)(2,1)}, u32[]{:S(2)}) %copy-start.3) | copy-done | bytes 262168
  59.1 0.0 copy-start.4
  59.1 0.9 %copy-done.4 = bf16[512,256]{1,0:T(8,128)(2,1)S(1)} copy-done((bf16[512,256]{1,0:T(8,128)(2,1)S(1)}, bf16[512,256]{1,0:T(8,128)(2,1)}, u32[]{:S(2)}) %copy-start.4) | copy-done | bytes 262168
  60.1 1.4 %shard_map.138 = (bf16[512,256]{1,0:T(8,128)(2,1)}, bf16[512,256]{1,0:T(8,128)(2,1)}, f32[512,256]{1,0:T(8,128)}, f32[512,256]{1,0:T(8,128)}, f32[512,256]{1,0:T(8,128)}) custom-call(bf16[512,256]{1,0:T(8,128)(2,1)S(1)} %copy-done, bf16[512,256]{1,0:T(8,128)(2,1)S(1)} %copy-done.1, bf16[512,256]{1,0:T(8,128)(2,1)S(1)} %copy-done.2, ...), custom_call_target="tpu_custom_call" | custom-call | tf_op jit(solution)/shard_map/pallas_call | solution.py:609
Async XLA Ops:
  55.3 1.0 %copy-start = (bf16[512,256]{1,0:T(8,128)(2,1)S(1)}, bf16[512,256]{1,0:T(8,128)(2,1)}, u32[]{:S(2)}) copy-start(bf16[512,256]{1,0:T(8,128)(2,1)} %get-tuple-element.10.refs_0_) | copy-start | bytes 786436
  56.3 0.9 %copy-start.1 = (bf16[512,256]{1,0:T(8,128)(2,1)S(1)}, bf16[512,256]{1,0:T(8,128)(2,1)}, u32[]{:S(2)}) copy-start(bf16[512,256]{1,0:T(8,128)(2,1)} %get-tuple-element.11.refs_1_) | copy-start | bytes 786436
  57.2 0.9 %copy-start.2 = (bf16[512,256]{1,0:T(8,128)(2,1)S(1)}, bf16[512,256]{1,0:T(8,128)(2,1)}, u32[]{:S(2)}) copy-start(bf16[512,256]{1,0:T(8,128)(2,1)} %get-tuple-element.12.refs_2_) | copy-start | bytes 786436
  58.2 0.9 %copy-start.3 = (bf16[512,256]{1,0:T(8,128)(2,1)S(1)}, bf16[512,256]{1,0:T(8,128)(2,1)}, u32[]{:S(2)}) copy-start(bf16[512,256]{1,0:T(8,128)(2,1)} %get-tuple-element.13.refs_3_) | copy-start | bytes 786436
  59.1 0.9 %copy-start.4 = (bf16[512,256]{1,0:T(8,128)(2,1)S(1)}, bf16[512,256]{1,0:T(8,128)(2,1)}, u32[]{:S(2)}) copy-start(bf16[512,256]{1,0:T(8,128)(2,1)} %get-tuple-element.14.refs_4_) | copy-start | bytes 786436

commit v3 on v2

--- a/solution.py
+++ b/solution.py
@@ -182,14 +182,15 @@
 
 def fused_kernel(
     n_lat, n_mesh,
-    grid_ref, mesh_ref, we_ref, wp_ref, wd_ref, dst_ref, count_ref, src_ref, pi_ref, cot_ref,
-    gg_ref, gm_ref, gwe_ref, gwp_ref, gwd_ref,
+    grid_hbm, mesh_hbm, we_hbm, wp_hbm, wd_hbm, dst_ref, count_ref, src_ref, pi_ref, cot_hbm,
+    gg_hbm, gm_hbm, gwe_hbm, gwp_hbm, gwd_hbm,
+    mesh_ref, cot_ref, gg_ref, gwp_ref, gwd_ref, s_in, s_out,
     gfull, wef, wpf, wdf, stage, psall, pst, idt, enc_m, enc_t, dec_m, inc_a, inc_t,
     halo_out, halo_in, own_win, sg_enc, one, ddec, sg_proc, pmsg, two, dpd, dtwo, dtwo_b, dpp,
     gmesh, dpe, dwin, rs_src, rs_own, rs_in, ag,
     s_f, r_f, s_p, r_p, s_h, r_h, s_z, r_z, s_x, r_x, s_c, r_c, s_rs, r_rs, s_ag, r_ag,
 ):
-    rows, half = grid_ref.shape
+    rows, half = cot_ref.shape
     shard = mesh_ref.shape[0]
     home = shard // n_lat
     bands = n_lat * n_mesh
@@ -213,6 +214,17 @@
     def band_at(index):
         return {"lat": index // n_mesh, "mesh": lax.rem(index, n_mesh)}
 
+    loads = [
+        pltpu.make_async_copy(s, t, s_in.at[i])
+        for i, (s, t) in enumerate(
+            (
+                (cot_hbm, cot_ref), (grid_hbm, gfull.at[:, mine]), (we_hbm, wef.at[:, mine]),
+                (mesh_hbm, mesh_ref), (wp_hbm, wpf.at[:, mine]), (wd_hbm, wdf.at[:, mine]),
+            )
+        )
+    ]
+    for copy in loads:
+        copy.start()
     barrier = pltpu.get_barrier_semaphore()
     for d in range(1, bands):
         pl.semaphore_signal(
@@ -245,15 +257,12 @@
             target[r:r + step, :] = acc.astype(BF)
 
     one_hot(dec_m, dec_ids)
+    loads[0].wait()
     dec_win = mm(dec_m[...], cot_ref[...]) / KD
     halo_out[0] = dec_win[2 * home:, :].astype(BF)
     halo_out[1] = dec_win[:home, :].astype(BF)
     own_win[0] = dec_win[home:2 * home, :]
     one_hot(enc_m, enc_ids)
-    gfull[:, mine] = grid_ref[...]
-    wef[:, mine] = we_ref[...]
-    wpf[:, mine] = wp_ref[...]
-    wdf[:, mine] = wd_ref[...]
     psall[m] = stage[...]
 
     @pl.when(b == 0)
@@ -266,13 +275,13 @@
         halo_in[1] = jnp.zeros((home, half), BF)
         halo_in[3] = jnp.zeros((home, half), BF)
 
+    for copy in loads[1:]:
+        copy.wait()
     pl.semaphore_wait(barrier, bands)
 
     wides = [
-        remote(s, t.at[:, mine], s_f.at[i], r_f.at[i], feat=1 - f)
-        for i, (s, t) in enumerate(
-            ((grid_ref, gfull), (we_ref, wef), (wp_ref, wpf), (wd_ref, wdf))
-        )
+        remote(t.at[:, mine], t.at[:, mine], s_f.at[i], r_f.at[i], feat=1 - f)
+        for i, t in enumerate((gfull, wef, wpf, wdf))
     ]
     indices = [
         remote(stage, psall.at[m], s_p.at[e - 1], r_p.at[e - 1], mesh=lax.rem(m + e, n_mesh))
@@ -315,11 +324,13 @@
             halo(i, False).wait_send()
 
     halo_start(0)
-    for copy in indices + wides[1:]:
+    for copy in indices:
         copy.start()
 
     wides[0].wait_recv()
-    pre = mm(gfull[...], we_ref[...])
+    for copy in wides[1:]:
+        copy.start()
+    pre = mm(gfull[...], wef[:, mine])
     enc_win = mm(enc_m[...], (pre * sigm(pre)).astype(BF)) * factor
     halo_out[2] = enc_win[2 * home:, :].astype(BF)
     halo_out[3] = enc_win[:home, :].astype(BF)
@@ -429,16 +440,17 @@
     home_rows = pl.ds(pl.multiple_of(m * shard + l * home, home), home)
     halo_recv(0)
     ddec[home_rows, mine] = banded(0).astype(BF)
+    spread_own(ddec, 1)
+    lax.fori_loop(0, rows // step, build_e, 0)
     halo_recv(1)
     mesh_home = mesh_ref[pl.ds(pl.multiple_of(l * home, home), home), :].astype(F32)
     one[home_rows, mine] = (mesh_home + banded(1)).astype(BF)
     spread_own(one, 0)
     lax.fori_loop(0, nodes // step, build_a, 0)
     spread_lat(one, 0)
-    spread_own(ddec, 1)
+    spread_lat(ddec, 1)
     spread_mesh(one, 0)
     lax.fori_loop(0, nodes // step, build_t, 0)
-    spread_lat(ddec, 1)
     wides[1].wait_recv()
     wides[2].wait_recv()
     wides[3].wait_recv()
@@ -467,7 +479,6 @@
     pre_all = mm(gfull[...], wef[...])
     sig_all = sigm(pre_all)
     sg_enc[...] = sig_all * (1.0 + pre_all * (1.0 - sig_all))
-    lax.fori_loop(0, rows // step, build_e, 0)
     spread_done(ddec, 1)
 
     def decode(at):
@@ -488,6 +499,13 @@
 
     tiles(third)
 
+    def store(i, source, target):
+        copy = pltpu.make_async_copy(source, target, s_out.at[i])
+        copy.start()
+        return copy
+
+    own_rows = pl.ds(pl.multiple_of(m * shard, shard), shard)
+    stores = [store(0, gmesh.at[own_rows, mine], gm_hbm)]
     for j in range(3):
         at = jnp.clip(b + j - 1, 0, bands - 1)
         first = pl.multiple_of(lax.rem(at, n_mesh) * shard + at // n_mesh * home, home)
@@ -511,7 +529,9 @@
         )
         scatter[-1].start()
     gwd_ref[...] = mm(two[...], dpd[:, mine], TN).astype(BF)
+    stores.append(store(1, gwd_ref, gwd_hbm))
     gwp_ref[...] = mm(one[...], dpp[:, mine], TN).astype(BF)
+    stores.append(store(2, gwp_ref, gwp_hbm))
     total = rs_own[part(b), :]
     for d in range(1, bands):
         scatter[d - 1].wait_recv()
@@ -527,7 +547,7 @@
         gather[-1].start()
     terms = mm(dpe[...], wef[mine, :], NT)
     gg_ref[...] = (cot_ref[...].astype(F32) + terms).astype(BF)
-    gm_ref[...] = gmesh[pl.ds(pl.multiple_of(m * shard, shard), shard), mine]
+    stores.append(store(3, gg_ref, gg_hbm))
     for copy in wides + indices:
         copy.wait_send()
     halo_sent(0)
@@ -541,9 +561,11 @@
         remote(
             view, view, s_ag.at[d - 1], r_ag.at[d - 1], **band_at(lax.rem(b + d, bands))
         ).wait_recv()
-    gwe_ref[...] = ag[...]
+    stores.append(store(4, ag, gwe_hbm))
     for copy in gather:
         copy.wait_send()
+    for copy in stores:
+        copy.wait()
 
 
 def widen_kernel(*refs):
@@ -566,6 +588,7 @@
     v = pltpu.VMEM
     dma = pltpu.SemaphoreType.DMA
     vmem = pl.BlockSpec(memory_space=pltpu.VMEM)
+    hbm = pl.BlockSpec(memory_space=pl.ANY)
     shaped = jax.ShapeDtypeStruct
     parts = pl.pallas_call(
         functools.partial(fused_kernel, n_lat, n_mesh),
@@ -576,9 +599,11 @@
             shaped((wide, half), BF),
             shaped((wide, half), BF),
         ),
-        in_specs=[vmem] * 10,
-        out_specs=(vmem,) * 5,
+        in_specs=[hbm] * 5 + [vmem] * 4 + [hbm],
+        out_specs=(hbm,) * 5,
         scratch_shapes=[
+            v((shard, half), BF), v((rows, half), BF), v((rows, half), BF), v((wide, half), BF),
+            v((wide, half), BF), dma((6,)), dma((5,)),
             v((rows, wide), BF), v((wide, wide), BF), v((wide, wide), BF), v((wide, wide), BF),
             v((8, shard), jnp.int32), v((n_mesh, 8, shard), jnp.int32), v((nodes, 8), F32), v((rows, 8), F32),
             v((win, rows), BF), v((rows, win), BF), v((win, rows), BF),
@@ -617,7 +642,7 @@
         ),
         in_specs=[vmem] * 5,
         out_specs=(vmem,) * 5,
-        compiler_params=pltpu.CompilerParams(vmem_limit_bytes=16 * 1024 * 1024),
+        compiler_params=pltpu.CompilerParams(vmem_limit_bytes=60 * 1024 * 1024),
     )(*parts))
 
 

time: 61.8 us -> 58 us (0.939)
  local copies, waits for them, and re-layouts: 4.74 us -> 0 us
  Pallas kernels: 56.1 us -> 57.1 us
    unnamed x10 -> x0, local copies, waits for them, and re-layouts: 4.74 us -> none
    pallas_call x1, Pallas kernels: 1.42 us -> 2.6 us  [local_fused(): pl.pallas_call(widen_kernel, out_shape=(shaped((rows, half), BF), shaped(...]
where the time goes in v3:
time: 58 us; the launch traced here: 57.7 us
  Pallas kernels  57.1 us (98%)
  between operations  0.64 us (1%)
    pallas_call x1, Pallas kernels, local_fused(): pl.pallas_call(functools.partial(fused_kernel, n_lat, n_mesh), out_shape=...  54.5 us
    pallas_call x1, Pallas kernels, local_fused(): pl.pallas_call(widen_kernel, out_shape=(shaped((rows, half), BF), shaped(...  2.6 us

profile of v3, /device:TPU:0, one launch (start us, length us, event | category | flops | bytes accessed | tf_op | source)
XLA Modules:
  0.0 57.7 jit_solution(3775358895589636512)
XLA Ops:
  0.6 54.5 %shard_map.137 = (bf16[512,256]{1,0:T(8,128)(2,1)}, bf16[512,256]{1,0:T(8,128)(2,1)}, bf16[512,256]{1,0:T(8,128)(2,1)}, bf16[512,256]{1,0:T(8,128)(2,1)}, bf16[512,256]{1,0:T(8,128)(2,1)}) custom-call(bf16[512,256]{1,0:T(8,128)(2,1)} %grid_hbm.1, bf16[512,256]{1,0:T(8,128)(2,1)} %mesh_hbm.1, bf16[512,256]{1,0:T(8,128)(2,1)} %we_hbm.1, ...), custom_call_target="tpu_custom_call" | custom-call | flops 2684354560 | bytes 2097152 | tf_op jit(solution)/shard_map/pallas_call | solution.py:593
  55.1 2.6 %shard_map.138 = (bf16[512,256]{1,0:T(8,128)(2,1)}, bf16[512,256]{1,0:T(8,128)(2,1)}, f32[512,256]{1,0:T(8,128)}, f32[512,256]{1,0:T(8,128)}, f32[512,256]{1,0:T(8,128)}) custom-call(bf16[512,256]{1,0:T(8,128)(2,1)} %get-tuple-element.10.refs_0_, bf16[512,256]{1,0:T(8,128)(2,1)} %get-tuple-element.11.refs_1_, bf16[512,256]{1,0:T(8,128)(2,1)} %get-tuple-element.12.refs_2_, ...), custom_call_target="tpu_custom_call" | custom-call | tf_op jit(solution)/shard_map/pallas_call | solution.py:634

commit v4 on v3

--- a/solution.py
+++ b/solution.py
@@ -187,8 +187,8 @@
     mesh_ref, cot_ref, gg_ref, gwp_ref, gwd_ref, s_in, s_out,
     gfull, wef, wpf, wdf, stage, psall, pst, idt, enc_m, enc_t, dec_m, inc_a, inc_t,
     halo_out, halo_in, own_win, sg_enc, one, ddec, sg_proc, pmsg, two, dpd, dtwo, dtwo_b, dpp,
-    gmesh, dpe, dwin, rs_src, rs_own, rs_in, ag,
-    s_f, r_f, s_p, r_p, s_h, r_h, s_z, r_z, s_x, r_x, s_c, r_c, s_rs, r_rs, s_ag, r_ag,
+    gmesh, dpe, dwin, rs_src, rs_own, rs_x, rs_out, rs_in, ag,
+    s_f, r_f, s_p, r_p, s_h, r_h, s_z, r_z, s_x, r_x, s_c, r_c, s_rx, r_rx, s_rs, r_rs, s_ag, r_ag, s_ax, r_ax,
 ):
     rows, half = cot_ref.shape
     shard = mesh_ref.shape[0]
@@ -515,52 +515,89 @@
     rs_own[...] = weight
     rs_src[...] = weight.astype(BF)
 
-    def part(index):
-        return pl.ds(pl.multiple_of(index * chunk, chunk), chunk)
+    def part(at_l, at_m):
+        return pl.ds(pl.multiple_of((at_m * n_lat + at_l) * chunk, chunk), chunk)
+
+    def ahead(d):
+        return lax.rem(l + d, n_lat)
+
+    def behind(d):
+        return lax.rem(l + n_lat - d, n_lat)
+
+    def across(d, e):
+        to = lax.rem(m + e, n_mesh)
+        return remote(
+            rs_src.at[part(ahead(d), to), :], rs_x.at[d, e - 1], s_rx.at[d, e - 1],
+            r_rx.at[d, e - 1], mesh=to,
+        )
+
+    pieces = list(range(1, n_lat)) + [0]
+    crossing = {(d, e): across(d, e) for d in pieces for e in range(1, n_mesh)}
+    for copy in crossing.values():
+        copy.start()
+    gwd_ref[...] = mm(two[...], dpd[:, mine], TN).astype(BF)
+    stores.append(store(1, gwd_ref, gwd_hbm))
+
+    def column_sum(d):
+        total = rs_own[part(ahead(d), m), :]
+        for e in range(1, n_mesh):
+            crossing[d, e].wait_recv()
+            total = total + rs_x[d, e - 1].astype(F32)
+        return total
 
     scatter, gather = [], []
-    for d in range(1, bands):
-        to = lax.rem(b + d, bands)
+    for d in range(1, n_lat):
+        rs_out[d - 1] = column_sum(d).astype(BF)
         scatter.append(
             remote(
-                rs_src.at[part(to), :], rs_in.at[d - 1], s_rs.at[d - 1], r_rs.at[d - 1],
-                **band_at(to),
+                rs_out.at[d - 1], rs_in.at[d - 1], s_rs.at[d - 1], r_rs.at[d - 1], lat=ahead(d)
             )
         )
         scatter[-1].start()
-    gwd_ref[...] = mm(two[...], dpd[:, mine], TN).astype(BF)
-    stores.append(store(1, gwd_ref, gwd_hbm))
     gwp_ref[...] = mm(one[...], dpp[:, mine], TN).astype(BF)
     stores.append(store(2, gwp_ref, gwp_hbm))
-    total = rs_own[part(b), :]
-    for d in range(1, bands):
+    total = column_sum(0)
+    for d in range(1, n_lat):
         scatter[d - 1].wait_recv()
         total = total + rs_in[d - 1].astype(F32)
-    ag[part(b), :] = total.astype(BF)
-    for d in range(1, bands):
-        gather.append(
-            remote(
-                ag.at[part(b), :], ag.at[part(b), :], s_ag.at[d - 1], r_ag.at[d - 1],
-                **band_at(lax.rem(b + d, bands)),
-            )
-        )
-        gather[-1].start()
+    ag[part(l, m), :] = total.astype(BF)
+
+    def ag_lat(d, view):
+        return remote(view, view, s_ag.at[d - 1], r_ag.at[d - 1], lat=ahead(d))
+
+    def ag_mesh(d, e, view):
+        return remote(
+            view, view, s_ax.at[d, e - 1], r_ax.at[d, e - 1], mesh=lax.rem(m + e, n_mesh)
+        )
+
+    own_part = ag.at[part(l, m), :]
+    for d in range(1, n_lat):
+        gather.append(ag_lat(d, own_part))
+    for e in range(1, n_mesh):
+        gather.append(ag_mesh(0, e, own_part))
+    for copy in gather:
+        copy.start()
     terms = mm(dpe[...], wef[mine, :], NT)
     gg_ref[...] = (cot_ref[...].astype(F32) + terms).astype(BF)
     stores.append(store(3, gg_ref, gg_hbm))
+    for d in range(1, n_lat):
+        view = ag.at[part(behind(d), m), :]
+        ag_lat(d, view).wait_recv()
+        for e in range(1, n_mesh):
+            gather.append(ag_mesh(d, e, view))
+            gather[-1].start()
     for copy in wides + indices:
         copy.wait_send()
     halo_sent(0)
     halo_sent(1)
     spread_sent(one, 0)
     spread_sent(ddec, 1)
-    for copy in scatter:
+    for copy in list(crossing.values()) + scatter:
         copy.wait_send()
-    for d in range(1, bands):
-        view = ag.at[part(lax.rem(b + bands - d, bands)), :]
-        remote(
-            view, view, s_ag.at[d - 1], r_ag.at[d - 1], **band_at(lax.rem(b + d, bands))
-        ).wait_recv()
+    for d in range(n_lat):
+        for e in range(1, n_mesh):
+            at_m = lax.rem(m + n_mesh - e, n_mesh)
+            ag_mesh(d, e, ag.at[part(behind(d), at_m), :]).wait_recv()
     stores.append(store(4, ag, gwe_hbm))
     for copy in gather:
         copy.wait_send()
@@ -615,13 +652,17 @@
             v((nodes, wide), F32), v((nodes, wide), BF), v((nodes, wide), BF),
             v((nodes, wide), BF), v((rows, wide), BF), v((win, wide), BF),
             v((wide, half), BF), v((wide, half), F32),
-            v((bands - 1, wide // bands, half), BF), v((wide, half), BF),
+            v((n_lat, n_mesh - 1, wide // bands, half), BF),
+            v((n_lat - 1, wide // bands, half), BF), v((n_lat - 1, wide // bands, half), BF),
+            v((wide, half), BF),
             dma((4,)), dma((4,)), dma((n_mesh - 1,)), dma((n_mesh - 1,)),
             dma((4,)), dma((4,)),
             dma((2, n_lat - 1)), dma((2, n_lat - 1)),
             dma((2, n_lat, n_mesh - 1)), dma((2, n_lat, n_mesh - 1)),
             dma((2, n_lat, n_mesh)), dma((2, n_lat, n_mesh)),
-            dma((bands - 1,)), dma((bands - 1,)), dma((bands - 1,)), dma((bands - 1,)),
+            dma((n_lat, n_mesh - 1)), dma((n_lat, n_mesh - 1)),
+            dma((n_lat - 1,)), dma((n_lat - 1,)), dma((n_lat - 1,)), dma((n_lat - 1,)),
+            dma((n_lat, n_mesh - 1)), dma((n_lat, n_mesh - 1)),
         ],
         compiler_params=pltpu.CompilerParams(
             collective_id=0, has_side_effects=True, vmem_limit_bytes=56 * 1024 * 1024

time: 58 us -> 60.4 us (1.041)
  Pallas kernels: 57.1 us -> 59.5 us
    pallas_call x1, Pallas kernels: 54.5 us -> 56.9 us  [local_fused(): pl.pallas_call(functools.partial(fused_kernel, n_lat, n_mesh), out_shape=...]
where the time goes in v4:
time: 60.4 us; the launch traced here: 60.2 us
  Pallas kernels  59.5 us (99%)
  between operations  0.64 us (1%)
    pallas_call x1, Pallas kernels, local_fused(): pl.pallas_call(functools.partial(fused_kernel, n_lat, n_mesh), out_shape=...  56.9 us
    pallas_call x1, Pallas kernels, local_fused(): pl.pallas_call(widen_kernel, out_shape=(shaped((rows, half), BF), shaped(...  2.6 us

profile of v4, /device:TPU:0, one launch (start us, length us, event | category | flops | bytes accessed | tf_op | source)
XLA Modules:
  0.0 60.2 jit_solution(18414246099586770711)
XLA Ops:
  0.6 56.9 %shard_map.137 = (bf16[512,256]{1,0:T(8,128)(2,1)}, bf16[512,256]{1,0:T(8,128)(2,1)}, bf16[512,256]{1,0:T(8,128)(2,1)}, bf16[512,256]{1,0:T(8,128)(2,1)}, bf16[512,256]{1,0:T(8,128)(2,1)}) custom-call(bf16[512,256]{1,0:T(8,128)(2,1)} %grid_hbm.1, bf16[512,256]{1,0:T(8,128)(2,1)} %mesh_hbm.1, bf16[512,256]{1,0:T(8,128)(2,1)} %we_hbm.1, ...), custom_call_target="tpu_custom_call" | custom-call | flops 2684354560 | bytes 2097152 | tf_op jit(solution)/shard_map/pallas_call | solution.py:630
  57.6 2.6 %shard_map.138 = (bf16[512,256]{1,0:T(8,128)(2,1)}, bf16[512,256]{1,0:T(8,128)(2,1)}, f32[512,256]{1,0:T(8,128)}, f32[512,256]{1,0:T(8,128)}, f32[512,256]{1,0:T(8,128)}) custom-call(bf16[512,256]{1,0:T(8,128)(2,1)} %get-tuple-element.10.refs_0_, bf16[512,256]{1,0:T(8,128)(2,1)} %get-tuple-element.11.refs_1_, bf16[512,256]{1,0:T(8,128)(2,1)} %get-tuple-element.12.refs_2_, ...), custom_call_target="tpu_custom_call" | custom-call | tf_op jit(solution)/shard_map/pallas_call | solution.py:675

commit v5 on v3

--- a/solution.py
+++ b/solution.py
@@ -185,7 +185,7 @@
     grid_hbm, mesh_hbm, we_hbm, wp_hbm, wd_hbm, dst_ref, count_ref, src_ref, pi_ref, cot_hbm,
     gg_hbm, gm_hbm, gwe_hbm, gwp_hbm, gwd_hbm,
     mesh_ref, cot_ref, gg_ref, gwp_ref, gwd_ref, s_in, s_out,
-    gfull, wef, wpf, wdf, stage, psall, pst, idt, enc_m, enc_t, dec_m, inc_a, inc_t,
+    grid_t, gfull, wef, wpf, wdf, stage, psall, pst, idt, enc_m, enc_t, dec_m, inc_a, inc_t,
     halo_out, halo_in, own_win, sg_enc, one, ddec, sg_proc, pmsg, two, dpd, dtwo, dtwo_b, dpp,
     gmesh, dpe, dwin, rs_src, rs_own, rs_in, ag,
     s_f, r_f, s_p, r_p, s_h, r_h, s_z, r_z, s_x, r_x, s_c, r_c, s_rs, r_rs, s_ag, r_ag,
@@ -451,6 +451,7 @@
     spread_lat(ddec, 1)
     spread_mesh(one, 0)
     lax.fori_loop(0, nodes // step, build_t, 0)
+    grid_t[...] = gfull[...].T
     wides[1].wait_recv()
     wides[2].wait_recv()
     wides[3].wait_recv()
@@ -510,8 +511,13 @@
         at = jnp.clip(b + j - 1, 0, bands - 1)
         first = pl.multiple_of(lax.rem(at, n_mesh) * shard + at // n_mesh * home, home)
         dwin[j * home:(j + 1) * home, :] = gmesh[pl.ds(first, home), :]
-    dpe[...] = (mm(enc_t[...], dwin[...]) * factor * sg_enc[...]).astype(BF)
-    weight = mm(gfull[...], dpe[:, mine], TN)
+
+    def encode(cols):
+        total = mm(enc_t[...], dwin[:, cols]) * factor
+        dpe[:, cols] = (total * sg_enc[:, cols]).astype(BF)
+
+    encode(mine)
+    weight = mm(grid_t[...], dpe[:, mine])
     rs_own[...] = weight
     rs_src[...] = weight.astype(BF)
 
@@ -528,6 +534,7 @@
             )
         )
         scatter[-1].start()
+    encode(pl.ds(pl.multiple_of((1 - f) * half, half), half))
     gwd_ref[...] = mm(two[...], dpd[:, mine], TN).astype(BF)
     stores.append(store(1, gwd_ref, gwd_hbm))
     gwp_ref[...] = mm(one[...], dpp[:, mine], TN).astype(BF)
@@ -604,6 +611,7 @@
         scratch_shapes=[
             v((shard, half), BF), v((rows, half), BF), v((rows, half), BF), v((wide, half), BF),
             v((wide, half), BF), dma((6,)), dma((5,)),
+            v((wide, rows), BF),
             v((rows, wide), BF), v((wide, wide), BF), v((wide, wide), BF), v((wide, wide), BF),
             v((8, shard), jnp.int32), v((n_mesh, 8, shard), jnp.int32), v((nodes, 8), F32), v((rows, 8), F32),
             v((win, rows), BF), v((rows, win), BF), v((win, rows), BF),
@@ -631,6 +639,7 @@
             transcendentals=4 * nodes * wide,
         ),
     )(grid_in, mesh_in, w_enc, w_proc, w_dec, enc_dst.T, enc_count[None, :], dec_src.T, proc_src.T, cotangent)
+    sizes = (rows, shard, wide, wide, wide)
     return tuple(pl.pallas_call(
         widen_kernel,
         out_shape=(
@@ -640,8 +649,9 @@
             shaped((wide, half), F32),
             shaped((wide, half), F32),
         ),
-        in_specs=[vmem] * 5,
-        out_specs=(vmem,) * 5,
+        grid=(4,),
+        in_specs=[pl.BlockSpec((r // 4, half), lambda i: (i, 0)) for r in sizes],
+        out_specs=tuple(pl.BlockSpec((r // 4, half), lambda i: (i, 0)) for r in sizes),
         compiler_params=pltpu.CompilerParams(vmem_limit_bytes=60 * 1024 * 1024),
     )(*parts))
 

time: 58 us -> 59.2 us (1.021)
  Pallas kernels: 57.1 us -> 58.2 us
    pallas_call x1, Pallas kernels: 2.6 us -> 3.6 us  [local_fused(): pl.pallas_call(widen_kernel, out_shape=(shaped((rows, half), BF), shaped(...]
where the time goes in v5:
time: 59.2 us; the launch traced here: 58.8 us
  Pallas kernels  58.2 us (98%)
  between operations  0.64 us (1%)
    pallas_call x1, Pallas kernels, local_fused(): pl.pallas_call(functools.partial(fused_kernel, n_lat, n_mesh), out_shape=...  54.6 us
    pallas_call x1, Pallas kernels, local_fused(): pl.pallas_call(widen_kernel, out_shape=(shaped((rows, half), BF), shaped(...  3.6 us

profile of v5, /device:TPU:0, one launch (start us, length us, event | category | flops | bytes accessed | tf_op | source)
XLA Modules:
  0.0 58.8 jit_solution(4937122009767181466)
XLA Ops:
  0.6 54.6 %shard_map.137 = (bf16[512,256]{1,0:T(8,128)(2,1)}, bf16[512,256]{1,0:T(8,128)(2,1)}, bf16[512,256]{1,0:T(8,128)(2,1)}, bf16[512,256]{1,0:T(8,128)(2,1)}, bf16[512,256]{1,0:T(8,128)(2,1)}) custom-call(bf16[512,256]{1,0:T(8,128)(2,1)} %grid_hbm.1, bf16[512,256]{1,0:T(8,128)(2,1)} %mesh_hbm.1, bf16[512,256]{1,0:T(8,128)(2,1)} %we_hbm.1, ...), custom_call_target="tpu_custom_call" | custom-call | flops 2684354560 | bytes 2097152 | tf_op jit(solution)/shard_map/pallas_call | solution.py:600
  55.3 3.6 %shard_map.138 = (bf16[512,256]{1,0:T(8,128)(2,1)}, bf16[512,256]{1,0:T(8,128)(2,1)}, f32[512,256]{1,0:T(8,128)}, f32[512,256]{1,0:T(8,128)}, f32[512,256]{1,0:T(8,128)}) custom-call(bf16[512,256]{1,0:T(8,128)(2,1)} %get-tuple-element.10.refs_0_, bf16[512,256]{1,0:T(8,128)(2,1)} %get-tuple-element.11.refs_1_, bf16[512,256]{1,0:T(8,128)(2,1)} %get-tuple-element.12.refs_2_, ...), custom_call_target="tpu_custom_call" | custom-call | tf_op jit(solution)/shard_map/pallas_call | solution.py:643
